TPU v7x, 32 devices: a whole 2x2x4 slice. The times are simulated.
32 devices in a mesh: pipe: 2 (over y), dp: 4 (over z), tensor: 4 (over x, core).
Axes of the slice: x: 2, y: 2, z: 4, core: 2. Of those that a mesh axis runs over, the one named last changes fastest.
Arguments:
- tokens: bfloat16 [3072, 8192], P(('pipe', 'dp'), 'tensor'), parts along dimension 0, may hold values from -6 to 6
- pattern: int32 [128, 6], P('pipe'), parts along dimension 0, may hold values from 0 to 31, as said below
- blocks: bfloat16 [128, 6, 256, 256], P(('pipe', 'tensor'), None, 'dp'), parts along dimension 0, may hold values from -0.15625 to 0.15625
- left_factor: bfloat16 [16384, 512], P(('pipe', 'tensor'), 'dp'), parts along dimension 0, may hold values from -0.0625 to 0.0625
- right_factor: bfloat16 [1024, 16384], P(('pipe', 'dp'), 'tensor'), parts along dimension 0, may hold values from -0.25 to 0.25
- cotangent: bfloat16 [3072, 16384], P(('pipe', 'dp'), 'tensor'), parts along dimension 0, may hold values from -6 to 6
Outputs:
- hidden: bfloat16 [3072, 16384], P(('pipe', 'dp'), 'tensor'), parts along dimension 0
- token_grad: float32 [3072, 8192], P(('pipe', 'dp'), 'tensor'), parts along dimension 0
- block_grad: float32 [128, 6, 256, 256], P(('pipe', 'tensor'), None, 'dp'), parts along dimension 0
- left_grad: float32 [16384, 512], P(('pipe', 'tensor'), 'dp'), parts along dimension 0
- right_grad: float32 [1024, 16384], P(('pipe', 'dp'), 'tensor'), parts along dimension 0
There are 2 independent parts, one for each index of `pipe`. A program takes and returns all parts, laid end to end along the dimension named above; each array names one. Nothing has to cross between parts.
Inputs may be any that keep to these rules, and one draw needn't show every extreme that they name: `pattern`: row j lists the 6 input blocks feeding hidden block j: under a relabeling of the 32 input blocks drawn from the seed, they are the labels of (j mod 32) XOR s for s = 0 and then the powers of two below 32 in rising order; a row's entries are distinct.
All inputs are finite; a program needn't handle non-finite values.
Results may differ from a plain program's by a relative error of at most 0.017.
Values may be sent and summed in bfloat16 or wider, within the bound.
A program may use at most 256 MiB of HBM per device.

v0:
```python
import jax
import jax.numpy as jnp
from jax import lax
from jax.sharding import PartitionSpec as P

SQRT_HALF = 0.7071067811865476
INV_ROOT_TWO_PI = 0.3989422804014327


def gelu_parts(preact):
    normal_cdf = 0.5 * (1.0 + jax.scipy.special.erf(preact * SQRT_HALF))
    return (
        preact * normal_cdf,
        normal_cdf + preact * jnp.exp(-0.5 * preact * preact) * INV_ROOT_TWO_PI,
    )


def per_device(tokens, pattern, blocks, left_factor, right_factor, cotangent):
    tok_rows = tokens.shape[0]
    block_size = blocks.shape[3]
    local_cols = blocks.shape[0]
    slot_count = blocks.shape[1]
    full_tokens = lax.all_gather(tokens, "tensor", axis=1, tiled=True)
    block_count = full_tokens.shape[1] // block_size
    tensor_rank = lax.axis_index("tensor")
    local_pattern = lax.dynamic_slice_in_dim(pattern, tensor_rank * local_cols, local_cols, 0)
    picked = jnp.take(full_tokens.reshape(tok_rows, block_count, block_size), local_pattern, axis=1)
    inputs = picked
    butterfly = jnp.einsum(
        "tjkc,jkcd->tjd",
        inputs,
        lax.all_gather(blocks, "dp", axis=2, tiled=True),
        preferred_element_type=jnp.float32,
    )
    left_rows = lax.all_gather(left_factor, "dp", axis=1, tiled=True)
    whole_left = lax.all_gather(left_rows, "tensor", axis=0, tiled=True)
    rank_acts = jnp.dot(full_tokens, whole_left, preferred_element_type=jnp.float32).astype(
        jnp.bfloat16
    )
    inputs = rank_acts
    rank_part = jnp.dot(
        inputs,
        lax.all_gather(right_factor, "dp", axis=0, tiled=True),
        preferred_element_type=jnp.float32,
    )
    preact = butterfly.reshape(tok_rows, -1) + rank_part
    activated, slope_values = gelu_parts(preact)
    hidden = activated.astype(jnp.bfloat16)
    grad_pre = (cotangent.astype(jnp.float32) * slope_values).astype(jnp.bfloat16)
    rank_terms = lax.dot_general(
        grad_pre,
        lax.all_gather(right_factor, "dp", axis=0, tiled=True),
        (((1,), (1,)), ((), ())),
        preferred_element_type=jnp.float32,
    )
    rank_grad = lax.psum(rank_terms.astype(jnp.bfloat16), "tensor")
    right_term = lax.dot_general(
        rank_acts, grad_pre, (((0,), (0,)), ((), ())), preferred_element_type=jnp.float32
    )
    right_grad = lax.psum_scatter(
        right_term.astype(jnp.bfloat16), "dp", scatter_dimension=0, tiled=True
    ).astype(jnp.float32)
    left_term = lax.dot_general(
        tokens, rank_grad, (((0,), (0,)), ((), ())), preferred_element_type=jnp.float32
    )
    left_grad = lax.psum_scatter(
        left_term.astype(jnp.bfloat16), "dp", scatter_dimension=1, tiled=True
    ).astype(jnp.float32)
    grad_blocks = grad_pre.reshape(tok_rows, local_cols, block_size)
    block_term = jnp.einsum(
        "tjkc,tjd->jkcd", picked, grad_blocks, preferred_element_type=jnp.float32
    )
    block_grad = lax.psum_scatter(
        block_term.astype(jnp.bfloat16), "dp", scatter_dimension=2, tiled=True
    ).astype(jnp.float32)
    spread = jnp.einsum(
        "tjd,jkcd->tjkc",
        grad_blocks,
        lax.all_gather(blocks, "dp", axis=2, tiled=True),
        preferred_element_type=jnp.float32,
    )
    placed = (
        jnp.zeros((tok_rows, block_count, block_size), jnp.float32)
        .at[:, local_pattern.reshape(-1)]
        .add(spread.reshape(tok_rows, local_cols * slot_count, block_size))
    )
    token_part = lax.psum_scatter(
        placed.reshape(tok_rows, -1).astype(jnp.bfloat16), "tensor", scatter_dimension=1, tiled=True
    ).astype(jnp.float32)
    token_grad = token_part + lax.dot_general(
        rank_grad, left_rows, (((1,), (1,)), ((), ())), preferred_element_type=jnp.float32
    )
    return (hidden, token_grad, block_grad, left_grad, right_grad)


def solution(mesh):
    placed = (
        P(("pipe", "dp"), "tensor"),
        P("pipe", None),
        P(("pipe", "tensor"), None, "dp", None),
        P(("pipe", "tensor"), "dp"),
        P(("pipe", "dp"), "tensor"),
        P(("pipe", "dp"), "tensor"),
    )
    return jax.shard_map(
        per_device,
        mesh=mesh,
        in_specs=placed,
        out_specs=(
            P(("pipe", "dp"), "tensor"),
            P(("pipe", "dp"), "tensor"),
            P(("pipe", "tensor"), None, "dp", None),
            P(("pipe", "tensor"), "dp"),
            P(("pipe", "dp"), "tensor"),
        ),
        check_vma=False,
    )
```

profile of v0, /device:TPU:0, one launch (start us, length us, event | category | flops | bytes accessed | tf_op | source)
XLA Modules:
  0.0 936.8 jit_solution(5141369474184893608)
XLA Ops:
  7.2 0.0 copy-start.5
  7.2 0.0 all-gather.10.cloned.1.call-start
  7.2 0.7 all-gather.10.cloned.1.call-update
  7.9 0.0 all-gather.6.cloned.1.call-start
  8.0 2.6 copy.32
  10.5 0.0 all-gather.6.cloned.1.call-update
  10.6 0.0 all-gather.12.cloned.1.call-start
  10.6 47.9 %all-gather.10.cloned.1.call-done = bf16[2048,512]{1,0:T(8,128)(2,1)} async-done(((bf16[2048,128]{1,0:T(8,128)(2,1)}), bf16[2048,512]{1,0:T(8,128)(2,1)}) %all-gather.10.cloned.1.call-update) | async-done | bytes 2097168 | tf_op jit(solution)/shard_map/all_gather | solution.py:35
  58.5 0.0 all-gather.12.cloned.1.call-update
  58.6 0.0 all-gather.8.cloned.1.call-start
  58.6 0.5 all-gather.8.cloned.1.call-update
  59.1 0.0 all-gather.14.cloned.1.call-start
  59.2 0.5 all-gather.14.cloned.1.call-update
  59.7 0.0 all-reduce.2.cloned.1.call-start
  59.8 0.0 copy-done.5
  59.8 0.1 compare_and_fusion
  59.9 0.1 copy.31
  60.0 0.1 copy.33
  60.1 0.1 reshape.67
  60.2 45.2 %all-gather.6.cloned.1.call-done = bf16[384,8192]{0,1:T(8,128)(2,1)} async-done(((bf16[384,2048]{0,1:T(8,128)(2,1)}), bf16[384,8192]{0,1:T(8,128)(2,1)}) %all-gather.6.cloned.1.call-update) | async-done | bytes 6291472 | tf_op jit(solution)/shard_map/all_gather | solution.py:23
  105.3 8.6 copy.34
  114.0 13.0 %gather_fusion = bf16[96,384,256]{2,1,0:T(8,128)(2,1)} fusion(bf16[384,32,256]{2,0,1:T(8,128)(2,1)} %copy.34, s32[1024]{0:T(1024)S(1)} %pad_clamp_fusion), kind=kCustom, calls=%fused_computation | custom fusion | bytes 37749120 | tf_op jit(solution)/shard_map/jit(_take)/gather | solution.py:27
  126.9 24.7 %copy.35 = bf16[16,6,384,256]{2,3,1,0:T(8,128)(2,1)} copy(bf16[16,6,384,256]{3,2,1,0:T(8,128)(2,1)} %bitcast.47) | data formatting | bytes 37748736 | tf_op jit(solution)/shard_map/jit(_take)/gather | solution.py:27
  151.6 13.6 %all-gather.12.cloned.1.call-done = bf16[8192,512]{1,0:T(8,128)(2,1)} async-done(((bf16[2048,512]{1,0:T(8,128)(2,1)}), bf16[8192,512]{1,0:T(8,128)(2,1)}) %all-gather.12.cloned.1.call-update) | async-done | bytes 8388624 | tf_op jit(solution)/shard_map/all_gather | solution.py:36
  165.2 8.6 convolution_convert_fusion.3
  173.8 211.0 %all-gather.8.cloned.1.call-done = bf16[16,6,256,256]{3,2,1,0:T(8,128)(2,1)} async-done(((bf16[16,6,64,256]{3,2,1,0:T(8,128)(2,1)}), bf16[16,6,256,256]{3,2,1,0:T(8,128)(2,1)}) %all-gather.8.cloned.1.call-update) | async-done | bytes 12582928 | tf_op jit(solution)/shard_map/all_gather | solution.py:32
  384.9 16.6 %fusion.2 = f32[16,384,256,1]{1,2,3,0:T(8,128)} fusion(bf16[16,6,256,256]{3,2,1,0:T(8,128)(2,1)} %all-gather.8.cloned.1.call-done, bf16[16,6,384,256]{2,3,1,0:T(8,128)(2,1)} %copy.35, pred[16,6]{1,0:T(8,128)(4,1)S(1)} %copy.31), kind=kOutput, calls=%fused_computation.4 | convolution fusion | flops 4841275392 | bytes 37748832 | tf_op jit(solution)/shard_map/tjkc,jkcd->tjd/dot_general | solution.py:29
  401.5 6.6 copy.37
  408.1 57.2 %all-gather.14.cloned.1.call-done = bf16[512,4096]{1,0:T(8,128)(2,1)} async-done(((bf16[128,4096]{1,0:T(8,128)(2,1)}), bf16[512,4096]{1,0:T(8,128)(2,1)}) %all-gather.14.cloned.1.call-update) | async-done | bytes 4194320 | tf_op jit(solution)/shard_map/all_gather | solution.py:43
  465.3 10.5 %fusion.14 = (bf16[384,4096]{1,0:T(8,128)(2,1)S(1)}, bf16[384,4096]{1,0:T(8,128)(2,1)}) fusion(bf16[384,4096]{1,0:T(8,128)(2,1)} %param.11, f32[384,4096]{1,0:T(8,128)} %copy.37, bf16[384,512]{1,0:T(8,128)(2,1)S(1)} %convolution_convert_fusion.3, bf16[512,4096]{1,0:T(8,128)(2,1)} %all-gather.14.cloned.1.call-done), kind=kOutput, calls=%fused_computation.16 | convolution fusion | flops 1632632832 | bytes 20316160 | tf_op jit(solution)/shard_map/dot_general | solution.py:41
  475.8 0.0 copy-done.6
  475.8 2.6 convolution_convert_fusion.2
  478.5 0.0 all-reduce.2.cloned.1.call-update
  478.5 0.2 reduce-scatter.9.cloned.1.call-start
  478.7 31.1 %all-reduce.2.cloned.1.call-done = bf16[384,512]{1,0:T(8,128)(2,1)} async-done(((bf16[384,512]{1,0:T(8,128)(2,1)}), bf16[384,512]{1,0:T(8,128)(2,1)}) %all-reduce.2.cloned.1.call-update) | async-done | bytes 393232 | tf_op jit(solution)/shard_map/psum | solution.py:56
  509.8 4.1 fusion.18
  513.9 0.0 reduce-scatter.9.cloned.1.call-update
  513.9 0.0 reduce-scatter.11.cloned.1.call-start
  514.0 0.0 copy-done.2
  514.0 4.4 convolution_convert_fusion
  518.4 0.0 reduce-scatter.11.cloned.1.call-update
  518.5 0.0 reduce-scatter.5.cloned.1.call-start
  518.5 0.1 copy.38
  518.6 0.1 reshape.62
  518.7 3.3 copy.52
  522.0 0.0 copy-start
  522.0 25.2 %fusion.16 = f32[16,384,6,256]{3,1,2,0:T(8,128)} fusion(bf16[16,6,256,256]{3,2,1,0:T(8,128)(2,1)} %all-gather.8.cloned.1.call-done, bf16[384,16,256,1]{2,1,0,3:T(8,128)(2,1)S(1)} %bitcast.50), kind=kOutput, calls=%fused_computation.25 | convolution fusion | flops 4831838208 | bytes 53477376 | tf_op jit(solution)/shard_map/tjd,jkcd->tjkc/dot_general | solution.py:76
  547.2 0.0 copy-done
  547.2 5.9 broadcast_in_dim.19
  553.1 90.2 %scatter_fusion = f32[384,32,256]{2,0,1:T(8,128)} fusion(f32[384,32,256]{2,0,1:T(8,128)} %broadcast_in_dim.19, s32[96]{0:T(128)S(1)} %fusion.19, f32[96,384,256]{2,1,0:T(8,128)} %bitcast.46), kind=kCustom, calls=%fused_computation.1 | custom fusion | flops 9437184 | bytes 113246592 | tf_op jit(solution)/shard_map/scatter-add | solution.py:85
  643.3 5.4 convert_bitcast_fusion
  648.8 3.5 copy.51
  652.3 0.0 reduce-scatter.5.cloned.1.call-update
  652.3 0.3 reduce-scatter.7.cloned.1.call-start
  652.6 1.6 copy-done.1
  654.2 15.2 %fusion.6 = bf16[16,6,256,256]{3,2,1,0:T(8,128)(2,1)} fusion(bf16[16,6,384,256]{2,3,1,0:T(8,128)(2,1)} %copy.35, pred[16,6]{1,0:T(8,128)(4,1)S(1)} %copy.31, bf16[384,16,256,1]{2,1,0,3:T(8,128)(2,1)S(1)} %bitcast.51), kind=kOutput, calls=%fused_computation.10 | convolution fusion | flops 4847566848 | bytes 34603104 | tf_op jit(solution)/shard_map/tjkc,tjd->jkcd/dot_general | solution.py:70
  669.4 0.0 reduce-scatter.7.cloned.1.call-update
  669.5 0.0 reduce-scatter.9.cloned.1.call-done
  669.5 2.4 copy.42
  671.9 2.9 convert_element_type.59
  674.8 35.7 %reduce-scatter.5.cloned.1.call-done = bf16[384,2048]{1,0:T(8,128)(2,1)} async-done(((bf16[384,8192]{1,0:T(8,128)(2,1)}), bf16[384,2048]{1,0:T(8,128)(2,1)}) %reduce-scatter.5.cloned.1.call-update) | async-done | bytes 1572880 | tf_op jit(solution)/shard_map/reduce_scatter | solution.py:87
  710.4 4.1 convert_add_fusion
  714.5 210.0 %reduce-scatter.7.cloned.1.call-done = bf16[16,6,64,256]{3,2,1,0:T(8,128)(2,1)} async-done(((bf16[16,6,256,256]{3,2,1,0:T(8,128)(2,1)}), bf16[16,6,64,256]{3,2,1,0:T(8,128)(2,1)}) %reduce-scatter.7.cloned.1.call-update) | async-done | bytes 3145744 | tf_op jit(solution)/shard_map/reduce_scatter | solution.py:73
  924.5 5.5 convert_element_type.54
  (11 shorter events, 0.0 us)
Async XLA Ops:
  7.2 52.6 %copy-start.5 = (s32[64,6]{0,1:T(8,128)S(1)}, s32[64,6]{0,1:T(8,128)}, u32[]{:S(2)}) copy-start(s32[64,6]{0,1:T(8,128)} %param.7) | copy-start | bytes 4612
  7.2 51.4 %all-gather.10.cloned.1.call-start = ((), (), s32[]{:S(2)}) async-start(), calls=%async_computation.6 | async-start | bytes 2621440 | tf_op jit(solution)/shard_map/all_gather | solution.py:35
  7.9 97.4 %all-gather.6.cloned.1.call-start = ((), (), s32[]{:S(2)}) async-start(), calls=%async_computation.4 | async-start | bytes 7864320 | tf_op jit(solution)/shard_map/all_gather | solution.py:23
  10.6 154.6 %all-gather.12.cloned.1.call-start = ((), (), s32[]{:S(2)}) async-start(), calls=%async_computation.7 | async-start | bytes 10485760 | tf_op jit(solution)/shard_map/all_gather | solution.py:36
  58.6 326.3 %all-gather.8.cloned.1.call-start = ((), (), s32[]{:S(2)}) async-start(), calls=%async_computation.5 | async-start | bytes 15728640 | tf_op jit(solution)/shard_map/all_gather | solution.py:32
  59.1 406.1 %all-gather.14.cloned.1.call-start = ((), (), s32[]{:S(2)}) async-start(), calls=%async_computation.8 | async-start | bytes 5242880 | tf_op jit(solution)/shard_map/all_gather | solution.py:43
  59.7 450.0 %all-reduce.2.cloned.1.call-start = ((), (), s32[]{:S(2)}) async-start(), calls=%async_computation.10 | async-start | bytes 786432 | tf_op jit(solution)/shard_map/psum | solution.py:56
  465.3 10.5 %copy-start.6 = (bf16[512,4096]{1,0:T(8,128)(2,1)S(1)}, bf16[512,4096]{1,0:T(8,128)(2,1)}, u32[]{:S(2)}) copy-start(bf16[512,4096]{1,0:T(8,128)(2,1)} %all-gather.14.cloned.1.call-done) | copy-start | bytes 12582916
  475.8 38.2 %copy-start.2 = (bf16[384,4096]{1,0:T(8,128)(2,1)}, bf16[384,4096]{1,0:T(8,128)(2,1)S(1)}, u32[]{:S(2)}) copy-start(bf16[384,4096]{1,0:T(8,128)(2,1)S(1)} %get-tuple-element.22) | copy-start | bytes 9437188
  478.5 191.0 %reduce-scatter.9.cloned.1.call-start = ((), (), s32[]{:S(2)}) async-start(), calls=%async_computation.12 | async-start | bytes 2621440 | tf_op jit(solution)/shard_map/reduce_scatter | solution.py:66
  513.9 157.9 %reduce-scatter.11.cloned.1.call-start = ((), (), s32[]{:S(2)}) async-start(), calls=%async_computation.13 | async-start | bytes 5242880 | tf_op jit(solution)/shard_map/reduce_scatter | solution.py:60
  518.5 192.0 %reduce-scatter.5.cloned.1.call-start = ((), (), s32[]{:S(2)}) async-start(), calls=%async_computation.9 | async-start | bytes 7864320 | tf_op jit(solution)/shard_map/reduce_scatter | solution.py:87
  522.0 25.2 %copy-start = (bf16[48,8,16,256]{3,2,1,0:T(8,128)(2,1)}, bf16[48,8,16,256]{3,2,1,0:T(8,128)(2,1)S(1)}, u32[]{:S(2)}) copy-start(bf16[48,8,16,256]{3,2,1,0:T(8,128)(2,1)S(1)} %copy.52) | copy-start | bytes 9437188
  652.3 1.9 copy-start.1
  652.3 272.2 %reduce-scatter.7.cloned.1.call-start = ((), (), s32[]{:S(2)}) async-start(), calls=%async_computation.11 | async-start | bytes 15728640 | tf_op jit(solution)/shard_map/reduce_scatter | solution.py:73
  669.4 41.0 %copy-start.3 = (bf16[2048,512]{1,0:T(8,128)(2,1)S(1)}, bf16[2048,512]{1,0:T(8,128)(2,1)}, u32[]{:S(2)}) copy-start(bf16[2048,512]{1,0:T(8,128)(2,1)} %all-gather.10.cloned.1.call-done) | copy-start | bytes 6291460
  669.4 41.0 %copy-start.4 = (bf16[384,512]{1,0:T(8,128)(2,1)S(1)}, bf16[384,512]{1,0:T(8,128)(2,1)}, u32[]{:S(2)}) copy-start(bf16[384,512]{1,0:T(8,128)(2,1)} %all-reduce.2.cloned.1.call-done) | copy-start | bytes 1179652
Sparse Core Ops, SparseCore 0:
  9.6 48.9 all-gather.9
  60.7 44.5 all-gather.5
  106.9 58.2 all-gather.11
  166.6 218.2 all-gather.7
  386.3 78.9 all-gather.13
  478.6 31.1 all-reduce.1
  514.0 43.8 reduce-scatter.8
  560.2 76.0 reduce-scatter.10
  652.4 57.9 reduce-scatter.4
  712.6 211.8 reduce-scatter.6
where the time goes:
time: 939 us; the launch traced here: 937 us
  waiting for transfers between devices  654 us (70%)
  other arithmetic  104 us (11%)
  matrix products  91.5 us (10%)
  local copies, waits for them, and re-layouts  72.6 us (8%)
  between operations  14.3 us (2%)
    all_gather x1, waiting for transfers between devices, per_device(): lax.all_gather(blocks, 'dp', axis=2, tiled=True)  211 us
    reduce_scatter x1, waiting for transfers between devices, per_device(): lax.psum_scatter(block_term.astype(jnp.bfloat16), 'dp', scatter_dimension...  210 us
    scatter-add x1, other arithmetic, per_device(): placed = jnp.zeros((tok_rows, block_count, block_size), jnp.float32).at[:...  90.2 us
    all_gather x1, waiting for transfers between devices, per_device(): lax.all_gather(right_factor, 'dp', axis=0, tiled=True)  57.2 us
    all_gather x1, waiting for transfers between devices, per_device(): left_rows = lax.all_gather(left_factor, 'dp', axis=1, tiled=True)  47.9 us
    all_gather x1, waiting for transfers between devices, per_device(): full_tokens = lax.all_gather(tokens, 'tensor', axis=1, tiled=True)  45.2 us
    gather x2, local copies, waits for them, and re-layouts, per_device(): jnp.take(full_tokens.reshape(tok_rows, block_count, block_size), local_pa...  37.6 us
    reduce_scatter x1, waiting for transfers between devices, per_device(): lax.psum_scatter(placed.reshape(tok_rows, -1).astype(jnp.bfloat16), 'tens...  35.7 us
  transfers between devices with their start and end apart: 10, of which 8 were waited for; matrix products, arithmetic and copies ran while one was open for 26% of the time, Pallas kernels for 0%

commit v1 on v0

--- a/solution.py
+++ b/solution.py
@@ -26,12 +26,20 @@
     local_pattern = lax.dynamic_slice_in_dim(pattern, tensor_rank * local_cols, local_cols, 0)
     picked = jnp.take(full_tokens.reshape(tok_rows, block_count, block_size), local_pattern, axis=1)
     inputs = picked
-    butterfly = jnp.einsum(
-        "tjkc,jkcd->tjd",
-        inputs,
-        lax.all_gather(blocks, "dp", axis=2, tiled=True),
-        preferred_element_type=jnp.float32,
-    )
+    count, here, span = (lax.axis_size("dp"), lax.axis_index("dp"), blocks.shape[2])
+    right = [(i, (i + 1) % count) for i in range(count)]
+    block, so_far = (blocks, None)
+    for step in range(count):
+        coming = lax.ppermute(block, "dp", right) if step < count - 1 else None
+        absorb = jnp.einsum(
+            "tjkc,jkcd->tjd",
+            lax.dynamic_slice_in_dim(inputs, (here - step) % count * span, block.shape[2], axis=3),
+            block,
+            preferred_element_type=jnp.float32,
+        )
+        so_far = absorb if so_far is None else so_far + absorb
+        block = coming
+    butterfly = so_far
     left_rows = lax.all_gather(left_factor, "dp", axis=1, tiled=True)
     whole_left = lax.all_gather(left_rows, "tensor", axis=0, tiled=True)
     rank_acts = jnp.dot(full_tokens, whole_left, preferred_element_type=jnp.float32).astype(

time: 939 us -> 1040 us (1.11)
  waiting for transfers between devices: 654 us -> 729 us
  other arithmetic: 104 us -> 118 us
    ppermute x0 -> x3, waiting for transfers between devices: none -> 190 us  [per_device(): coming = lax.ppermute(block, 'dp', right) if step < count - 1 else None]
    all_gather x1, waiting for transfers between devices: 57.2 us -> 0.02 us  [per_device(): lax.all_gather(right_factor, 'dp', axis=0, tiled=True)]
    all_gather x1, waiting for transfers between devices: 45.2 us -> 0.01 us  [per_device(): full_tokens = lax.all_gather(tokens, 'tensor', axis=1, tiled=True)]
    dot_general x1 -> x4, matrix products: 16.6 us -> 34.7 us  [per_device(): jnp.einsum('tjkc,jkcd->tjd', lax.dynamic_slice_in_dim(inputs, (here - ste...]
    all_gather x1, waiting for transfers between devices: 13.6 us -> 0.01 us  [per_device(): whole_left = lax.all_gather(left_rows, 'tensor', axis=0, tiled=True)]
  transfers between devices with their start and end apart: 10 -> 13, of which waited for: 8 -> 8; matrix products, arithmetic and copies ran while one was open for 26% -> 26% of each run, Pallas kernels for 0% -> 0%
where the time goes in v1:
time: 1040 us
  waiting for transfers between devices  729 us (70%)
  other arithmetic  118 us (11%)
  matrix products  96.7 us (9%)
  local copies, waits for them, and re-layouts  72.3 us (7%)
  between operations  14.4 us (1%)
    reduce_scatter x1, waiting for transfers between devices, per_device(): lax.psum_scatter(block_term.astype(jnp.bfloat16), 'dp', scatter_dimension...  210 us
    all_gather x1, waiting for transfers between devices, per_device(): lax.all_gather(blocks, 'dp', axis=2, tiled=True)  208 us
    ppermute x3, waiting for transfers between devices, per_device(): coming = lax.ppermute(block, 'dp', right) if step < count - 1 else None  190 us
    scatter-add x1, other arithmetic, per_device(): placed = jnp.zeros((tok_rows, block_count, block_size), jnp.float32).at[:...  90.1 us
    all_gather x1, waiting for transfers between devices, per_device(): left_rows = lax.all_gather(left_factor, 'dp', axis=1, tiled=True)  47.8 us
    reduce_scatter x1, waiting for transfers between devices, per_device(): lax.psum_scatter(placed.reshape(tok_rows, -1).astype(jnp.bfloat16), 'tens...  39.3 us
    gather x2, local copies, waits for them, and re-layouts, per_device(): jnp.take(full_tokens.reshape(tok_rows, block_count, block_size), local_pa...  36.6 us
    dot_general x4, matrix products, per_device(): jnp.einsum('tjkc,jkcd->tjd', lax.dynamic_slice_in_dim(inputs, (here - ste...  34.7 us
  transfers between devices with their start and end apart: 13, of which 8 were waited for; matrix products, arithmetic and copies ran while one was open for 26% of the time, Pallas kernels for 0%

profile of v1, /device:TPU:0, one launch (start us, length us, event | category | flops | bytes accessed | tf_op | source)
XLA Modules:
  0.0 1040.4 jit_solution(16582622014454873347)
XLA Ops:
  7.2 0.0 all-gather.8.cloned.1.call-start
  7.2 0.7 all-gather.8.cloned.1.call-update
  7.9 0.0 all-gather.6.cloned.1.call-start
  8.0 2.7 copy.29
  10.7 0.0 all-gather.6.cloned.1.call-update
  10.7 0.0 all-gather.10.cloned.1.call-start
  10.8 47.8 %all-gather.8.cloned.1.call-done = bf16[2048,512]{1,0:T(8,128)(2,1)} async-done(((bf16[2048,128]{1,0:T(8,128)(2,1)}), bf16[2048,512]{1,0:T(8,128)(2,1)}) %all-gather.8.cloned.1.call-update) | async-done | bytes 2097168 | tf_op jit(solution)/shard_map/all_gather | solution.py:43
  58.6 0.0 all-gather.10.cloned.1.call-update
  58.6 0.0 all-gather.12.cloned.1.call-start
  58.6 0.2 collective-permute-start
  58.9 70.9 %collective-permute-done = bf16[16,6,64,256]{3,2,1,0:T(8,128)(2,1)} collective-permute-done((bf16[16,6,64,256]{3,2,1,0:T(8,128)(2,1)S(1)}, bf16[16,6,64,256]{3,2,1,0:T(8,128)(2,1)}, u32[]{:S(2)}, u32[]{:S(2)}) %collective-permute-start) | collective-permute-done | bytes 3145760 | tf_op jit(solution)/shard_map/ppermute | solution.py:33
  129.8 0.0 all-gather.12.cloned.1.call-update
  129.8 0.0 all-reduce.2.cloned.1.call-start
  129.9 0.1 compare_and_fusion
  130.0 0.1 copy.28
  130.1 0.1 copy.30
  130.2 0.1 reshape.67
  130.3 93.0 %collective-permute-done.1 = bf16[16,6,64,256]{3,2,1,0:T(8,128)(2,1)} collective-permute-done((bf16[16,6,64,256]{3,2,1,0:T(8,128)(2,1)}, bf16[16,6,64,256]{3,2,1,0:T(8,128)(2,1)}, u32[]{:S(2)}, u32[]{:S(2)}) %collective-permute-start.1) | collective-permute-done | bytes 3145760 | tf_op jit(solution)/shard_map/ppermute | solution.py:33
  223.4 9.0 collective-permute-start.2
  232.3 8.6 copy.31
  241.0 11.9 %gather_fusion = bf16[96,384,256]{2,1,0:T(8,128)(2,1)} fusion(bf16[384,32,256]{2,0,1:T(8,128)(2,1)} %copy.31, s32[1024]{0:T(1024)S(1)} %pad_clamp_fusion), kind=kCustom, calls=%fused_computation | custom fusion | bytes 37749120 | tf_op jit(solution)/shard_map/jit(_take)/gather | solution.py:27
  252.9 24.6 %copy.32 = bf16[96,384,256]{1,2,0:T(8,128)(2,1)} copy(bf16[96,384,256]{2,1,0:T(8,128)(2,1)} %gather_fusion) | data formatting | bytes 37748736 | tf_op jit(solution)/shard_map/jit(_take)/gather | solution.py:27
  277.6 10.3 broadcast_select_fusion
  287.9 5.3 fusion.17
  293.2 9.1 fusion.13
  302.3 6.7 fusion.15
  309.0 26.1 %collective-permute-done.2 = bf16[16,6,64,256]{3,2,1,0:T(8,128)(2,1)} collective-permute-done((bf16[16,6,64,256]{3,2,1,0:T(8,128)(2,1)}, bf16[16,6,64,256]{3,2,1,0:T(8,128)(2,1)}, u32[]{:S(2)}, u32[]{:S(2)}) %collective-permute-start.2) | collective-permute-done | bytes 3145760 | tf_op jit(solution)/shard_map/ppermute | solution.py:33
  335.1 13.6 %bitcast_add_fusion = f32[16,384,256]{1,2,0:T(8,128)} fusion(f32[16,384,256,1]{1,2,3,0:T(8,128)} %fusion.13, f32[16,384,256,1]{1,2,3,0:T(8,128)} %fusion.15, f32[16,384,256,1]{1,2,3,0:T(8,128)} %fusion.17, bf16[16,6,64,256]{3,2,1,0:T(8,128)(2,1)} %collective-permute-done.2, bf16[16,6,384,256]{2,3,1,0:T(8,128)(2,1)} %copy-done, s32[]{:T(128)S(6)} %select_n.63), kind=kOutput, calls=%fused_computation.13 | convolution fusion | flops 1212678144 | bytes 33030148 | tf_op jit(solution)/shard_map/tjkc,jkcd->tjd/dot_general | solution.py:34
  348.8 6.6 copy.33
  355.4 8.6 convolution_convert_fusion.3
  364.0 0.0 all-gather.12.cloned.1.call-done
  364.1 4.1 fusion.34
  368.2 0.8 copy-done.6
  369.0 4.2 fusion.10
  373.3 2.6 convolution_convert_fusion.2
  375.8 0.0 all-reduce.2.cloned.1.call-update
  375.8 0.0 all-gather.14.cloned.1.call-start
  375.9 0.5 all-gather.14.cloned.1.call-update
  376.4 0.0 reduce-scatter.9.cloned.1.call-start
  376.5 32.1 %all-reduce.2.cloned.1.call-done = bf16[384,512]{1,0:T(8,128)(2,1)} async-done(((bf16[384,512]{1,0:T(8,128)(2,1)}), bf16[384,512]{1,0:T(8,128)(2,1)}) %all-reduce.2.cloned.1.call-update) | async-done | bytes 393232 | tf_op jit(solution)/shard_map/psum | solution.py:64
  408.6 4.1 fusion.26
  412.7 0.0 reduce-scatter.9.cloned.1.call-update
  412.8 0.0 reduce-scatter.11.cloned.1.call-start
  412.8 4.4 convolution_convert_fusion
  417.2 0.0 reduce-scatter.5.cloned.1.call-start
  417.3 0.1 copy.34
  417.4 0.1 reshape.62
  417.5 2.8 copy.50
  420.3 208.2 %all-gather.14.cloned.1.call-done = bf16[16,6,256,256]{3,2,1,0:T(8,128)(2,1)} async-done(((bf16[16,6,64,256]{3,2,1,0:T(8,128)(2,1)}), bf16[16,6,256,256]{3,2,1,0:T(8,128)(2,1)}) %all-gather.14.cloned.1.call-update) | async-done | bytes 12582928 | tf_op jit(solution)/shard_map/all_gather | solution.py:87
  628.4 20.3 %fusion.24 = f32[16,384,6,256]{3,1,2,0:T(8,128)} fusion(bf16[16,6,256,256]{3,2,1,0:T(8,128)(2,1)} %all-gather.14.cloned.1.call-done, bf16[384,16,256,1]{2,1,0,3:T(8,128)(2,1)} %bitcast.80), kind=kOutput, calls=%fused_computation.35 | convolution fusion | flops 4831838208 | bytes 53477376 | tf_op jit(solution)/shard_map/tjd,jkcd->tjkc/dot_general | solution.py:84
  648.7 6.0 broadcast_in_dim.19
  654.7 90.1 %scatter_fusion = f32[384,32,256]{2,0,1:T(8,128)} fusion(f32[384,32,256]{2,0,1:T(8,128)} %broadcast_in_dim.19, s32[96]{0:T(128)S(1)} %fusion.33, f32[96,384,256]{2,1,0:T(8,128)} %bitcast.74), kind=kCustom, calls=%fused_computation.1 | custom fusion | flops 9437184 | bytes 113246592 | tf_op jit(solution)/shard_map/scatter-add | solution.py:93
  744.8 5.5 convert_bitcast_fusion
  750.3 3.5 copy.49
  753.8 0.0 reduce-scatter.7.cloned.1.call-start
  753.9 1.8 copy-done.2
  755.7 13.8 %fusion.2 = bf16[16,6,256,256]{3,2,1,0:T(8,128)(2,1)} fusion(bf16[16,6,384,256]{2,3,1,0:T(8,128)(2,1)} %copy-done, bf16[384,16,256,1]{2,1,0,3:T(8,128)(2,1)S(1)} %bitcast.81), kind=kOutput, calls=%fused_computation.6 | convolution fusion | flops 4838129664 | bytes 34603008 | tf_op jit(solution)/shard_map/tjkc,tjd->jkcd/dot_general | solution.py:78
  769.5 0.0 reduce-scatter.9.cloned.1.call-done
  769.6 2.4 copy.38
  771.9 2.8 convert_element_type.59
  774.7 39.3 %reduce-scatter.5.cloned.1.call-done = bf16[384,2048]{1,0:T(8,128)(2,1)} async-done(((bf16[384,8192]{1,0:T(8,128)(2,1)}), bf16[384,2048]{1,0:T(8,128)(2,1)}) %reduce-scatter.5.cloned.1.call-update) | async-done | bytes 1572880 | tf_op jit(solution)/shard_map/reduce_scatter | solution.py:95
  814.0 4.1 convert_add_fusion
  818.1 210.0 %reduce-scatter.7.cloned.1.call-done = bf16[16,6,64,256]{3,2,1,0:T(8,128)(2,1)} async-done(((bf16[16,6,256,256]{3,2,1,0:T(8,128)(2,1)}), bf16[16,6,64,256]{3,2,1,0:T(8,128)(2,1)}) %reduce-scatter.7.cloned.1.call-update) | async-done | bytes 3145744 | tf_op jit(solution)/shard_map/reduce_scatter | solution.py:81
  1028.1 5.5 convert_element_type.54
  (26 shorter events, 0.1 us)
Async XLA Ops:
  7.2 51.5 %copy-start.3 = (bf16[16,6,64,256]{3,2,1,0:T(8,128)(2,1)S(1)}, bf16[16,6,64,256]{3,2,1,0:T(8,128)(2,1)}, u32[]{:S(2)}) copy-start(bf16[16,6,64,256]{3,2,1,0:T(8,128)(2,1)} %param.8) | copy-start | bytes 9437188
  7.2 122.7 %copy-start.8 = (s32[64,6]{0,1:T(8,128)S(1)}, s32[64,6]{0,1:T(8,128)}, u32[]{:S(2)}) copy-start(s32[64,6]{0,1:T(8,128)} %param.7) | copy-start | bytes 4612
  7.2 51.4 %all-gather.8.cloned.1.call-start = ((), (), s32[]{:S(2)}) async-start(), calls=%async_computation.5 | async-start | bytes 2621440 | tf_op jit(solution)/shard_map/all_gather | solution.py:43
  7.9 224.4 %all-gather.6.cloned.1.call-start = ((), (), s32[]{:S(2)}) async-start(), calls=%async_computation.4 | async-start | bytes 7864320 | tf_op jit(solution)/shard_map/all_gather | solution.py:23
  10.7 344.7 %all-gather.10.cloned.1.call-start = ((), (), s32[]{:S(2)}) async-start(), calls=%async_computation.6 | async-start | bytes 10485760 | tf_op jit(solution)/shard_map/all_gather | solution.py:44
  58.6 305.5 %all-gather.12.cloned.1.call-start = ((), (), s32[]{:S(2)}) async-start(), calls=%async_computation.7 | async-start | bytes 5242880 | tf_op jit(solution)/shard_map/all_gather | solution.py:51
  58.6 71.1 %collective-permute-start = (bf16[16,6,64,256]{3,2,1,0:T(8,128)(2,1)S(1)}, bf16[16,6,64,256]{3,2,1,0:T(8,128)(2,1)}, u32[]{:S(2)}, u32[]{:S(2)}) collective-permute-start(bf16[16,6,64,256]{3,2,1,0:T(8,128)(2,1)S(1)} %copy-done.3), channel_id=1, source_target_pairs={{0,4},{4,8},{8,12},{12,0},{1,5},{5,9},{9,13},{13,1},{2,6},{6,10},{... | collective-permute-start | bytes 9437192 | tf_op jit(solution)/shard_map/ppermute | solution.py:33
  129.8 93.6 %collective-permute-start.1 = (bf16[16,6,64,256]{3,2,1,0:T(8,128)(2,1)}, bf16[16,6,64,256]{3,2,1,0:T(8,128)(2,1)}, u32[]{:S(2)}, u32[]{:S(2)}) collective-permute-start(bf16[16,6,64,256]{3,2,1,0:T(8,128)(2,1)} %collective-permute-done), channel_id=1, source_target_pairs={{0,4},{4,8},{8,12},{12,0},{1,5},{5,9},{9,13},{13,1},{2,6},{6,10},{... | collective-permute-start | bytes 9437192 | tf_op jit(solution)/shard_map/ppermute | solution.py:33
  129.8 278.8 %all-reduce.2.cloned.1.call-start = ((), (), s32[]{:S(2)}) async-start(), calls=%async_computation.10 | async-start | bytes 786432 | tf_op jit(solution)/shard_map/psum | solution.py:64
  223.4 111.7 %collective-permute-start.2 = (bf16[16,6,64,256]{3,2,1,0:T(8,128)(2,1)}, bf16[16,6,64,256]{3,2,1,0:T(8,128)(2,1)}, u32[]{:S(2)}, u32[]{:S(2)}) collective-permute-start(bf16[16,6,64,256]{3,2,1,0:T(8,128)(2,1)} %collective-permute-done.1), channel_id=1, source_target_pairs={{0,4},{4,8},{8,12},{12,0},{1,5},{5,9},{9,13},{13,1},{2,6},{6,10},{... | collective-permute-start | bytes 9437192 | tf_op jit(solution)/shard_map/ppermute | solution.py:33
  287.9 14.4 %copy-start = (bf16[16,6,384,256]{2,3,1,0:T(8,128)(2,1)}, bf16[16,6,384,256]{2,3,1,0:T(8,128)(2,1)S(1)}, u32[]{:S(2)}) copy-start(bf16[16,6,384,256]{2,3,1,0:T(8,128)(2,1)S(1)} %broadcast_select_fusion) | copy-start | bytes 56623108
  364.1 4.2 copy-start.1
  364.1 5.0 copy-start.6
  369.0 4.2 copy-start.5
  375.8 252.6 %all-gather.14.cloned.1.call-start = ((), (), s32[]{:S(2)}) async-start(), calls=%async_computation.8 | async-start | bytes 15728640 | tf_op jit(solution)/shard_map/all_gather | solution.py:87
  376.4 393.1 %reduce-scatter.9.cloned.1.call-start = ((), (), s32[]{:S(2)}) async-start(), calls=%async_computation.12 | async-start | bytes 2621440 | tf_op jit(solution)/shard_map/reduce_scatter | solution.py:74
  412.8 359.2 %reduce-scatter.11.cloned.1.call-start = ((), (), s32[]{:S(2)}) async-start(), calls=%async_computation.13 | async-start | bytes 5242880 | tf_op jit(solution)/shard_map/reduce_scatter | solution.py:68
  417.2 396.8 %reduce-scatter.5.cloned.1.call-start = ((), (), s32[]{:S(2)}) async-start(), calls=%async_computation.9 | async-start | bytes 7864320 | tf_op jit(solution)/shard_map/reduce_scatter | solution.py:95
  753.8 1.9 copy-start.2
  753.8 274.3 %reduce-scatter.7.cloned.1.call-start = ((), (), s32[]{:S(2)}) async-start(), calls=%async_computation.11 | async-start | bytes 15728640 | tf_op jit(solution)/shard_map/reduce_scatter | solution.py:81
  769.5 44.5 %copy-start.4 = (bf16[2048,512]{1,0:T(8,128)(2,1)S(1)}, bf16[2048,512]{1,0:T(8,128)(2,1)}, u32[]{:S(2)}) copy-start(bf16[2048,512]{1,0:T(8,128)(2,1)} %all-gather.8.cloned.1.call-done) | copy-start | bytes 6291460
  769.5 44.5 %copy-start.7 = (bf16[384,512]{1,0:T(8,128)(2,1)S(1)}, bf16[384,512]{1,0:T(8,128)(2,1)}, u32[]{:S(2)}) copy-start(bf16[384,512]{1,0:T(8,128)(2,1)} %all-reduce.2.cloned.1.call-done) | copy-start | bytes 1179652
Sparse Core Ops, SparseCore 0:
  9.6 48.9 all-gather.7
  60.7 44.5 all-gather.5
  106.9 58.2 all-gather.9
  166.6 135.4 all-gather.11
  376.0 32.6 all-reduce.1
  410.1 218.2 all-gather.13
  631.4 41.9 reduce-scatter.8
  675.7 76.0 reduce-scatter.10
  755.1 58.8 reduce-scatter.4
  816.2 211.8 reduce-scatter.6
